TPU v7x, 256 devices: a whole 4x4x8 slice. The times are simulated.
256 devices in a mesh: segment: 16 (over x, y), mp: 16 (over z, core).
Axes of the slice: x: 4, y: 4, z: 8, core: 2. Of those that a mesh axis runs over, the one named last changes fastest.
Arguments:
- noise_init: float32 [8192, 64], P('segment'), may hold values from -6 to 6
- step_noise: float32 [4, 8192, 64], P(None, 'segment'), may hold values from -6 to 6
- assign: int32 [128], P('segment'), may hold values from 0 to 31
- slot_map: int32 [128], replicated, may hold values from 0 to 255, as said below
- prompt_embed: bfloat16 [32, 1536], P('segment', 'mp'), may hold values from -6 to 6
- time_vec: bfloat16 [1536], P('mp'), may hold values from -6 to 6
- w_in: bfloat16 [64, 1536], P('segment', 'mp'), may hold values from -0.75 to 0.75
- ln_gain: bfloat16 [1536], P('mp'), may hold values from 0.099609375 to 1.8984375
- w_up: bfloat16 [1536, 6144], P('segment', 'mp'), may hold values from -0.15625 to 0.15625
- w_down: bfloat16 [6144, 1536], P('mp', 'segment'), may hold values from -0.109375 to 0.109375
- w_out: bfloat16 [1536, 64], P('mp', 'segment'), may hold values from -0.15625 to 0.15625
- conv_in_w: bfloat16 [3, 3, 16, 512], replicated, may hold values from -0.5 to 0.5
- gn_gain: float32 [512], replicated, may hold values from 0.1 to 1.9
- conv_mid_w: bfloat16 [3, 3, 512, 512], replicated, may hold values from -0.09375 to 0.09375
Outputs:
- latents: float32 [8192, 64], P('segment')
- decoded: bfloat16 [256, 2, 128, 512], P('segment', None, 'mp')
Inputs may be any that keep to these rules, and one draw needn't show every extreme that they name: `slot_map`: different samples have different slots. Decoder section d owns slots d * 16 to (d + 1) * 16 - 1; in every draw some section has all of its 16 slots filled, and slots 0 and 255 are used.
All inputs are finite; a program needn't handle non-finite values.
Results may differ from a plain program's by a relative error of at most 0.015.
Values may be sent and summed in bfloat16 or wider, within the bound.
A program may use at most 64 MiB of HBM per device.

v0:
```python
import math
import jax
import jax.numpy as jnp
from jax import lax
from jax.sharding import PartitionSpec as P

LAT_CH = 16
VC = 512
GROUPS = 32
STEPS = 4
NOISE_SCALE = 0.5
LATENT_SCALE = 1.0 / 1.5305
EPSILON = 1e-06


def split_up(value, dim, devices):
    before, after = (value.shape[:dim], value.shape[dim + 1 :])
    return jnp.moveaxis(value.reshape(*before, devices, -1, *after), dim, 0)


def sum_at_owner(value, axis, dim):
    blocks = split_up(value, dim, lax.axis_size(axis))
    arrived = lax.all_to_all(blocks, axis, split_axis=0, concat_axis=0, tiled=True)
    return arrived.astype(jnp.float32).sum(axis=0)


def sent_to_all(value, axis):
    copies = jnp.broadcast_to(value, (lax.axis_size(axis), *value.shape))
    return lax.all_to_all(copies, axis, split_axis=0, concat_axis=0, tiled=True)


def taken_together(value, axis):
    return sent_to_all(value, axis).astype(jnp.float32).sum(axis=0)


def joined_along(blocks, dim):
    blocks = jnp.moveaxis(blocks, 0, dim)
    lengths = blocks.shape
    return blocks.reshape(*lengths[:dim], lengths[dim] * lengths[dim + 1], *lengths[dim + 2 :])


def gathered_copies(value, axis, dim):
    return joined_along(sent_to_all(value, axis), dim)


def conv_rows(padded, weight, col_count):
    accumulated = None
    for row_shift in range(3):
        for col_shift in range(3):
            window = padded[:, row_shift : row_shift + 2, col_shift : col_shift + col_count, :]
            product = jnp.einsum(
                "nrcv,vw->nrcw",
                window,
                weight[row_shift, col_shift],
                preferred_element_type=jnp.float32,
            )
            accumulated = product if accumulated is None else accumulated + product
    return accumulated


def decode_tile(latent_tile, mp_index, tile_cols, image_cols, conv_in_w, gn_gain, conv_mid_w):
    slot_rows = latent_tile.shape[0]
    padded = jnp.pad(latent_tile.astype(jnp.bfloat16), ((0, 0), (1, 1), (0, 0), (0, 0)))
    first_wide = conv_rows(padded, conv_in_w, tile_cols + 2)
    conv_first = first_wide[:, :, 1 : tile_cols + 1, :]
    per_group = VC // GROUPS
    grouped = conv_first.reshape(slot_rows, 2 * tile_cols, GROUPS, per_group)
    group_sum, group_square = lax.psum(
        (jnp.sum(grouped, axis=(1, 3)), jnp.sum(grouped * grouped, axis=(1, 3))), "mp"
    )
    entries = 2 * image_cols * per_group
    average = group_sum / entries
    variance = jnp.maximum(group_square / entries - average * average, 0.0)
    inv_spread = lax.rsqrt(variance + EPSILON)
    columns = mp_index * tile_cols - 1 + jnp.arange(tile_cols + 2, dtype=jnp.int32)
    inside = (columns >= 0) & (columns < image_cols)
    col_count = first_wide.shape[2]
    shaped = first_wide.reshape(slot_rows, 2, col_count, GROUPS, per_group)
    shaped = (shaped - average[:, None, None, :, None]) * inv_spread[:, None, None, :, None]
    act_wide = jnp.where(
        inside[None, None, :, None],
        jax.nn.silu(shaped.reshape(slot_rows, 2, col_count, VC) * gn_gain),
        0.0,
    ).astype(jnp.bfloat16)
    act_padded = jnp.pad(act_wide, ((0, 0), (1, 1), (0, 0), (0, 0)))
    return (conv_first + conv_rows(act_padded, conv_mid_w, tile_cols)).astype(jnp.bfloat16)


def full_front(
    latent_state,
    w_in_full,
    prompt_cond,
    time_full,
    gain_full,
    time_now,
    samples_here,
    tok_sample,
    tok_group,
):
    embedded = jnp.dot(
        latent_state.astype(jnp.bfloat16), w_in_full, preferred_element_type=jnp.float32
    )
    hidden_in = (embedded.reshape(samples_here, tok_sample, -1) + prompt_cond[:, None, :]).reshape(
        tok_group, -1
    ) + time_now * time_full.astype(jnp.float32)
    average = jnp.mean(hidden_in, axis=-1, keepdims=True)
    centered = hidden_in - average
    variance = jnp.mean(centered * centered, axis=-1, keepdims=True)
    normed = (centered * lax.rsqrt(variance + EPSILON) * gain_full.astype(jnp.float32)).astype(
        jnp.bfloat16
    )
    return (hidden_in, normed)


def per_device(
    noise_init,
    step_noise,
    assign,
    slot_map,
    prompt_embed,
    time_vec,
    w_in,
    ln_gain,
    w_up,
    w_down,
    w_out,
    conv_in_w,
    gn_gain,
    conv_mid_w,
):
    mp_count = lax.axis_size("mp")
    mp_index = lax.axis_index("mp")
    segment_index = lax.axis_index("segment")
    w_in_rows, w_up_rows, w_down_cols, w_out_cols, prompt_rows = (
        lax.all_gather(w_in, "segment", axis=0, tiled=True),
        lax.all_gather(w_up, "segment", axis=0, tiled=True),
        lax.all_gather(w_down, "segment", axis=1, tiled=True),
        lax.all_gather(w_out, "segment", axis=1, tiled=True),
        lax.all_gather(prompt_embed, "segment", axis=0, tiled=True),
    )
    samples_here = assign.shape[0]
    tok_group = noise_init.shape[0]
    tok_sample = tok_group // samples_here
    prompt_count = prompt_rows.shape[0]
    choose = (assign[:, None] == jnp.arange(prompt_count, dtype=jnp.int32)[None, :]).astype(
        jnp.bfloat16
    )
    step_size = 1.0 / STEPS
    noise_gain = NOISE_SCALE * math.sqrt(step_size)
    latent_state = noise_init
    w_in_full, prompt_full, time_full, gain_full = (
        lax.all_gather(w_in_rows, "mp", axis=1, tiled=True),
        lax.all_gather(prompt_rows, "mp", axis=1, tiled=True),
        lax.all_gather(time_vec, "mp", axis=0, tiled=True),
        lax.all_gather(ln_gain, "mp", axis=0, tiled=True),
    )
    prompt_cond = jnp.dot(choose, prompt_full, preferred_element_type=jnp.float32)
    feat_width = w_out_cols.shape[0]
    for step_index in range(STEPS):
        time_now = 1.0 - step_index * step_size
        hidden_in, normed = full_front(
            latent_state,
            w_in_full,
            prompt_cond,
            time_full,
            gain_full,
            time_now,
            samples_here,
            tok_sample,
            tok_group,
        )
        act = jax.nn.gelu(
            jnp.dot(normed, w_up_rows, preferred_element_type=jnp.float32), approximate=True
        ).astype(jnp.bfloat16)
        mlp_share = sum_at_owner(
            jnp.dot(act, w_down_cols, preferred_element_type=jnp.float32).astype(jnp.bfloat16),
            "mp",
            1,
        )
        hidden_part = lax.dynamic_slice_in_dim(hidden_in, mp_index * feat_width, feat_width, 1)
        partial_vel = jnp.dot(
            (hidden_part + mlp_share).astype(jnp.bfloat16),
            w_out_cols,
            preferred_element_type=jnp.float32,
        )
        velocity = taken_together(partial_vel.astype(jnp.bfloat16), "mp").astype(jnp.float32)
        latent_state = latent_state - step_size * velocity + noise_gain * step_noise[step_index]
    image_cols = 2 * tok_sample
    tile_cols = image_cols // mp_count
    images = (
        latent_state.reshape(samples_here, tok_sample, 2, 2, LAT_CH)
        .transpose(0, 2, 1, 3, 4)
        .reshape(samples_here, 2, image_cols, LAT_CH)
        * LATENT_SCALE
    )
    widened = jnp.pad(images, ((0, 0), (0, 0), (2, 2), (0, 0)))
    latent_tile = lax.dynamic_slice_in_dim(widened, mp_index * tile_cols, tile_cols + 4, 2)
    slot_count = 2 * samples_here
    first_slot = segment_index * slot_count
    slot_ids = first_slot + jnp.arange(slot_count, dtype=jnp.int32)
    own_feats = decode_tile(
        latent_tile, mp_index, tile_cols, image_cols, conv_in_w, gn_gain, conv_mid_w
    )
    slot_picks = (slot_map[None, :] == slot_ids[:, None]).astype(jnp.bfloat16)
    flat_feats = own_feats.reshape(samples_here, -1)
    placed = jnp.dot(
        slot_picks, gathered_copies(flat_feats, "segment", 0), preferred_element_type=jnp.float32
    )
    decoded = placed.astype(jnp.bfloat16).reshape(slot_count, 2, tile_cols, VC)
    return (latent_state, decoded)


def solution(mesh):
    return jax.shard_map(
        per_device,
        mesh=mesh,
        in_specs=(
            P("segment", None),
            P(None, "segment", None),
            P("segment"),
            P(),
            P("segment", "mp"),
            P("mp"),
            P("segment", "mp"),
            P("mp"),
            P("segment", "mp"),
            P("mp", "segment"),
            P("mp", "segment"),
            P(),
            P(),
            P(),
        ),
        out_specs=(P("segment", None), P("segment", None, "mp", None)),
        check_vma=False,
    )
```

profile of v0, /device:TPU:8, one launch (start us, length us, event | category | flops | bytes accessed | tf_op | source)
XLA Modules:
  0.0 554.9 jit_solution(1239499764776693210)
XLA Ops:
  12.3 29.7 %all-reduce.6 = (bf16[1536]{0:T(1024)(128)(2,1)S(1)}, bf16[1536]{0:T(1024)(128)(2,1)S(1)}) all-reduce(bf16[1536]{0:T(1024)(128)(2,1)S(1)} %dynamic-update-slice, bf16[1536]{0:T(1024)(128)(2,1)S(1)} %dynamic-update-slice.1), channel_id=1, replica_groups=mesh['segment'=16,'mp'=16] {'mp'}, use_global_device_ids=true, to_apply=%add.3 | all-reduce | flops 3072 | bytes 12288
  42.1 22.8 %all-gather = bf16[16,4,96]{2,1,0:T(4,128)(2,1)S(1)} all-gather(bf16[1,4,96]{2,1,0:T(4,128)(2,1)} %bitcast.242), channel_id=1, replica_groups=mesh['segment'=16,'mp'=16] {'segment'}, dimensions={0}, use_global_device_ids=true | all-gather | bytes 13056 | tf_op jit(solution)/shard_map/all_gather | solution.py:135
  64.9 14.9 %all-gather.1 = bf16[16,96,64]{1,2,0:T(8,128)(2,1)S(1)} all-gather(bf16[1,96,64]{1,2,0:T(8,128)(2,1)S(1)} %bitcast.240), channel_id=1, replica_groups=mesh['segment'=16,'mp'=16] {'mp'}, dimensions={0}, use_global_device_ids=true | all-gather | bytes 208896 | tf_op jit(solution)/shard_map/all_gather | solution.py:152
  80.2 18.4 %all-gather.2 = bf16[16,2,96]{2,1,0:T(2,128)(2,1)S(1)} all-gather(bf16[1,2,96]{2,1,0:T(2,128)(2,1)} %bitcast.244), channel_id=1, replica_groups=mesh['segment'=16,'mp'=16] {'segment'}, dimensions={0}, use_global_device_ids=true | all-gather | bytes 6528 | tf_op jit(solution)/shard_map/all_gather | solution.py:139
  98.6 16.4 %all-gather.3 = bf16[16,96,32]{1,2,0:T(8,128)(2,1)S(1)} all-gather(bf16[1,96,32]{1,2,0:T(8,128)(2,1)S(1)} %bitcast.241), channel_id=1, replica_groups=mesh['segment'=16,'mp'=16] {'mp'}, dimensions={0}, use_global_device_ids=true | all-gather | bytes 104448 | tf_op jit(solution)/shard_map/all_gather | solution.py:153
  118.2 4.8 convolution_convert_fusion.4
  125.6 4.4 all-to-all-start
  130.0 22.3 %all-gather.4 = bf16[16,4,96]{2,1,0:T(4,128)(2,1)S(1)} all-gather(bf16[1,4,96]{2,1,0:T(4,128)(2,1)S(1)} %bitcast.243), channel_id=1, replica_groups=mesh['segment'=16,'mp'=16] {'segment'}, dimensions={0}, use_global_device_ids=true | all-gather | bytes 13056 | tf_op jit(solution)/shard_map/all_gather | solution.py:138
  152.3 15.5 %all-to-all-done = bf16[16,512,96]{1,2,0:T(8,128)(2,1)} async-done(((bf16[16,512,96]{1,2,0:T(8,128)(2,1)}), bf16[16,512,96]{1,2,0:T(8,128)(2,1)}, u32[]{:S(2)}, u32[]{:S(2)}) %all-to-all-start) | async-done | bytes 1572896 | tf_op jit(solution)/shard_map/all_to_all | solution.py:23
  174.3 4.8 all-to-all-start.1
  180.4 25.4 %all-to-all-done.1 = bf16[16,512,64]{1,2,0:T(8,128)(2,1)S(1)} async-done(((bf16[16,512,64]{1,2,0:T(8,128)(2,1)}), bf16[16,512,64]{1,2,0:T(8,128)(2,1)S(1)}, u32[]{:S(2)}, u32[]{:S(2)}) %all-to-all-start.1) | async-done | bytes 1048608 | tf_op jit(solution)/shard_map/all_to_all | solution.py:29
  208.3 4.8 convolution_convert_fusion.3
  215.6 43.3 %all_to_all.45 = bf16[16,512,96]{1,2,0:T(8,128)(2,1)S(1)} all-to-all(bf16[16,512,96]{1,2,0:T(8,128)(2,1)} %bitcast.229), channel_id=1, replica_groups=mesh['segment'=16,'mp'=16] {'mp'}, dimensions={0} | all-to-all | bytes 3145728 | tf_op jit(solution)/shard_map/all_to_all | solution.py:23
  262.9 31.3 %all_to_all.46 = bf16[16,512,64]{1,2,0:T(8,128)(2,1)S(1)} all-to-all(bf16[16,512,64]{1,2,0:T(8,128)(2,1)S(1)} %broadcast_in_dim.19), channel_id=1, replica_groups=mesh['segment'=16,'mp'=16] {'mp'}, dimensions={0} | all-to-all | bytes 2097152 | tf_op jit(solution)/shard_map/all_to_all | solution.py:29
  295.6 4.8 convolution_convert_fusion.2
  303.0 42.8 %all_to_all.47 = bf16[16,512,96]{1,2,0:T(8,128)(2,1)S(1)} all-to-all(bf16[16,512,96]{1,2,0:T(8,128)(2,1)} %bitcast.230), channel_id=1, replica_groups=mesh['segment'=16,'mp'=16] {'mp'}, dimensions={0} | all-to-all | bytes 3145728 | tf_op jit(solution)/shard_map/all_to_all | solution.py:23
  349.8 31.1 %all_to_all.48 = bf16[16,512,64]{1,2,0:T(8,128)(2,1)S(1)} all-to-all(bf16[16,512,64]{1,2,0:T(8,128)(2,1)S(1)} %broadcast_in_dim.20), channel_id=1, replica_groups=mesh['segment'=16,'mp'=16] {'mp'}, dimensions={0} | all-to-all | bytes 2097152 | tf_op jit(solution)/shard_map/all_to_all | solution.py:29
  383.2 4.8 convolution_convert_fusion.1
  390.5 42.8 %all_to_all.49 = bf16[16,512,96]{1,2,0:T(8,128)(2,1)S(1)} all-to-all(bf16[16,512,96]{1,2,0:T(8,128)(2,1)} %bitcast.231), channel_id=1, replica_groups=mesh['segment'=16,'mp'=16] {'mp'}, dimensions={0} | all-to-all | bytes 3145728 | tf_op jit(solution)/shard_map/all_to_all | solution.py:23
  438.4 4.1 all-to-all-start.7
  442.5 26.6 %all-to-all-done.7 = bf16[16,512,64]{1,2,0:T(8,128)(2,1)S(1)} async-done(((bf16[16,512,64]{1,2,0:T(8,128)(2,1)}), bf16[16,512,64]{1,2,0:T(8,128)(2,1)S(1)}, u32[]{:S(2)}, u32[]{:S(2)}) %all-to-all-start.7) | async-done | bytes 1048608 | tf_op jit(solution)/shard_map/all_to_all | solution.py:29
  473.0 25.8 %all-reduce.5 = (f32[8,32]{1,0:T(8,128)S(1)}, f32[8,32]{1,0:T(8,128)S(1)}) all-reduce(f32[8,32]{1,0:T(8,128)S(1)} %reduce_sum.197, f32[8,32]{1,0:T(8,128)S(1)} %reduce_sum.194), channel_id=1, replica_groups=mesh['segment'=16,'mp'=16] {'mp'}, use_global_device_ids=true, to_apply=%region_21.22 | all-reduce | flops 512 | bytes 4096 | tf_op jit(solution)/shard_map/psum | solution.py:68
  512.6 7.5 %all-to-all-start.8 = ((bf16[16,8,8192]{2,1,0:T(8,128)(2,1)}), bf16[16,8,8192]{2,1,0:T(8,128)(2,1)S(1)}, u32[]{:S(2)}, u32[]{:S(2)}) async-start(bf16[16,8,8192]{2,1,0:T(8,128)(2,1)} %broadcast_in_dim.24), calls=%async_computation.8 | async-start | bytes 4194304 | tf_op jit(solution)/shard_map/all_to_all | solution.py:29
  520.2 26.7 %all-to-all-done.8 = bf16[16,8,8192]{2,1,0:T(8,128)(2,1)S(1)} async-done(((bf16[16,8,8192]{2,1,0:T(8,128)(2,1)}), bf16[16,8,8192]{2,1,0:T(8,128)(2,1)S(1)}, u32[]{:S(2)}, u32[]{:S(2)}) %all-to-all-start.8) | async-done | bytes 2097184 | tf_op jit(solution)/shard_map/all_to_all | solution.py:29
  (131 shorter events, 64.0 us)
Async XLA Ops:
  7.2 111.0 %all-gather.10.cloned.1.call-start = ((), (), s32[]{:S(2)}) async-start(), calls=%async_computation.10 | async-start | bytes 1253376 | tf_op jit(solution)/shard_map/all_gather | solution.py:137
  7.9 110.3 %all-gather.8.cloned.1.call-start = ((), (), s32[]{:S(2)}) async-start(), calls=%async_computation.9 | async-start | bytes 1253376 | tf_op jit(solution)/shard_map/all_gather | solution.py:136
  42.0 22.8 %copy-start.9 = (bf16[1536]{0:T(1024)(128)(2,1)}, bf16[1536]{0:T(1024)(128)(2,1)S(1)}, u32[]{:S(2)}) copy-start(bf16[1536]{0:T(1024)(128)(2,1)S(1)} %get-tuple-element.6) | copy-start | bytes 9220
  115.2 3.0 copy-start.10
  123.0 7.0 %copy-start.14 = (bf16[96,4]{0,1:T(4,128)(2,1)S(1)}, bf16[96,4]{0,1:T(4,128)(2,1)}, u32[]{:S(2)}) copy-start(bf16[96,4]{0,1:T(4,128)(2,1)} %param.24) | copy-start | bytes 2308
  125.6 42.3 %all-to-all-start = ((bf16[16,512,96]{1,2,0:T(8,128)(2,1)}), bf16[16,512,96]{1,2,0:T(8,128)(2,1)}, u32[]{:S(2)}, u32[]{:S(2)}) async-start(bf16[16,512,96]{1,2,0:T(8,128)(2,1)} %bitcast.228), calls=%async_computation | async-start | bytes 3145728 | tf_op jit(solution)/shard_map/all_to_all | solution.py:23
  170.2 35.7 %copy-start.2 = (f32[512,64]{0,1:T(8,128)S(1)}, f32[512,64]{0,1:T(8,128)}, u32[]{:S(2)}) copy-start(f32[512,64]{0,1:T(8,128)} %param.14) | copy-start | bytes 393220
  174.3 31.5 %all-to-all-start.1 = ((bf16[16,512,64]{1,2,0:T(8,128)(2,1)}), bf16[16,512,64]{1,2,0:T(8,128)(2,1)S(1)}, u32[]{:S(2)}, u32[]{:S(2)}) async-start(bf16[16,512,64]{1,2,0:T(8,128)(2,1)} %broadcast_in_dim.18), calls=%async_computation.1 | async-start | bytes 2097152 | tf_op jit(solution)/shard_map/all_to_all | solution.py:29
  205.9 1.7 copy-start.6
  207.6 0.7 copy-start.11
  261.5 32.8 %copy-start = (f32[4,512,64]{1,2,0:T(8,128)S(1)}, f32[4,512,64]{1,2,0:T(8,128)}, u32[]{:S(2)}) copy-start(f32[4,512,64]{1,2,0:T(8,128)} %param.15) | copy-start | bytes 1572868
  261.5 32.8 %copy-start.3 = (f32[512,64]{0,1:T(8,128)S(1)}, f32[512,64]{0,1:T(8,128)}, u32[]{:S(2)}) copy-start(f32[512,64]{0,1:T(8,128)} %param.14) | copy-start | bytes 393220
  261.5 32.8 %copy-start.7 = (f32[512,64]{0,1:T(8,128)S(1)}, f32[512,64]{0,1:T(8,128)}, u32[]{:S(2)}) copy-start(f32[512,64]{0,1:T(8,128)} %copy-done.6) | copy-start | bytes 393220
  381.0 1.7 copy-start.4
  381.1 2.1 copy-start.12
  434.2 35.0 %copy-start.5 = (f32[512,64]{0,1:T(8,128)S(1)}, f32[512,64]{0,1:T(8,128)}, u32[]{:S(2)}) copy-start(f32[512,64]{0,1:T(8,128)} %copy-done.4) | copy-start | bytes 393220
  437.3 32.0 %copy-start.1 = (f32[4,512,64]{1,2,0:T(8,128)S(1)}, f32[4,512,64]{1,2,0:T(8,128)}, u32[]{:S(2)}) copy-start(f32[4,512,64]{1,2,0:T(8,128)} %param.15) | copy-start | bytes 1572868
  437.3 33.3 %copy-start.8 = (bf16[3,3,16,512]{3,2,1,0:T(8,128)(2,1)S(1)}, bf16[3,3,16,512]{3,2,1,0:T(8,128)(2,1)}, u32[]{:S(2)}) copy-start(bf16[3,3,16,512]{3,2,1,0:T(8,128)(2,1)} %param.25) | copy-start | bytes 442372
  438.4 30.7 %all-to-all-start.7 = ((bf16[16,512,64]{1,2,0:T(8,128)(2,1)}), bf16[16,512,64]{1,2,0:T(8,128)(2,1)S(1)}, u32[]{:S(2)}, u32[]{:S(2)}) async-start(bf16[16,512,64]{1,2,0:T(8,128)(2,1)} %broadcast_in_dim.21), calls=%async_computation.7 | async-start | bytes 2097152 | tf_op jit(solution)/shard_map/all_to_all | solution.py:29
  471.6 27.6 %copy-start.13 = (f32[512]{0:T(512)S(1)}, f32[512]{0:T(512)}, u32[]{:S(2)}) copy-start(f32[512]{0:T(512)} %param.26) | copy-start | bytes 6148
  511.1 35.8 %copy-start.15 = (s32[128]{0:T(128)S(1)}, s32[128]{0:T(128)}, u32[]{:S(2)}) copy-start(s32[128]{0:T(128)} %param.17) | copy-start | bytes 1540
  512.6 34.2 %all-to-all-start.8 = ((bf16[16,8,8192]{2,1,0:T(8,128)(2,1)}), bf16[16,8,8192]{2,1,0:T(8,128)(2,1)S(1)}, u32[]{:S(2)}, u32[]{:S(2)}) async-start(bf16[16,8,8192]{2,1,0:T(8,128)(2,1)} %broadcast_in_dim.24), calls=%async_computation.8 | async-start | bytes 4194304 | tf_op jit(solution)/shard_map/all_to_all | solution.py:29
Sparse Core Ops, SparseCore 0:
  10.5 50.6 all-gather.9
  63.7 47.5 all-gather.7
where the time goes:
time: 557 us; the launch traced here: 555 us
  blocking collectives  342 us (61%)
  waiting for transfers between devices  95.6 us (17%)
  matrix products  44.1 us (8%)
  local copies, waits for them, and re-layouts  27.4 us (5%)
  starting transfers between devices  20.8 us (4%)
  between operations  15.3 us (3%)
  other arithmetic  10 us (2%)
    all_to_all x3, blocking collectives, sum_at_owner(): lax.all_to_all(blocks, axis, split_axis=0, concat_axis=0, tiled=True)  129 us
    all_to_all x3, waiting for transfers between devices, sent_to_all(): return lax.all_to_all(copies, axis, split_axis=0, concat_axis=0, tiled=True)  78.7 us
    all_to_all x2, blocking collectives, sent_to_all(): return lax.all_to_all(copies, axis, split_axis=0, concat_axis=0, tiled=True)  62.4 us
    unnamed x1, blocking collectives  29.7 us
    psum x1, blocking collectives, decode_tile(): lax.psum((jnp.sum(grouped, axis=(1, 3)), jnp.sum(grouped * grouped, axis=...  25.8 us
    all_gather x1, blocking collectives, per_device(): lax.all_gather(w_in, 'segment', axis=0, tiled=True)  22.8 us
    all_gather x1, blocking collectives, per_device(): lax.all_gather(w_out, 'segment', axis=1, tiled=True)  22.3 us
    dot_general x4, matrix products, per_device(): jnp.dot(act, w_down_cols, preferred_element_type=jnp.float32)  19 us
  transfers between devices with their start and end apart: 6, of which 4 were waited for; matrix products, arithmetic and copies ran while one was open for 1% of the time, Pallas kernels for 0%

commit v1 on v0

--- a/solution.py
+++ b/solution.py
@@ -11,6 +11,28 @@
 NOISE_SCALE = 0.5
 LATENT_SCALE = 1.0 / 1.5305
 EPSILON = 1e-06
+
+
+def in_order(tiles, dim):
+    shape = list(tiles.shape[1:])
+    shape[dim] *= tiles.shape[0]
+    return jnp.moveaxis(tiles, 0, dim).reshape(shape)
+
+
+def collect(x, axis, dim):
+    count = lax.axis_size(axis)
+    pairs = [(i, (i + 1) % count) for i in range(count)]
+    back = [(b, a) for a, b in pairs]
+    lower, upper = ([], [])
+    for turn in range(count - 1):
+        if turn % 2 == 0:
+            lower.append(lax.ppermute(lower[-1] if lower else x, axis, pairs))
+        else:
+            upper.append(lax.ppermute(upper[-1] if upper else x, axis, back))
+    blocks = jnp.stack([*lower[::-1], x, *upper])
+    shift = lax.axis_index(axis) - len(lower)
+    blocks = blocks[(jnp.arange(count) - shift) % count]
+    return in_order(blocks, dim)
 
 
 def split_up(value, dim, devices):
@@ -149,7 +171,7 @@
     noise_gain = NOISE_SCALE * math.sqrt(step_size)
     latent_state = noise_init
     w_in_full, prompt_full, time_full, gain_full = (
-        lax.all_gather(w_in_rows, "mp", axis=1, tiled=True),
+        collect(w_in_rows, "mp", 1),
         lax.all_gather(prompt_rows, "mp", axis=1, tiled=True),
         lax.all_gather(time_vec, "mp", axis=0, tiled=True),
         lax.all_gather(ln_gain, "mp", axis=0, tiled=True),

time: 557 us -> 587 us (1.054)
  blocking collectives: 342 us -> 325 us
  starting transfers between devices: 20.8 us -> 36.8 us
  local copies, waits for them, and re-layouts: 27.4 us -> 41.4 us
  other arithmetic: 10 us -> 19.8 us
  waiting for transfers between devices: 95.6 us -> 103 us
    ppermute x0 -> x15, starting transfers between devices: none -> 15.4 us  [the longest x7 15 us: collect(): upper.append(lax.ppermute(upper[-1] if upper else x, axis, back))]
    all_gather x1 -> x0, blocking collectives: 14.9 us -> none  [per_device(): lax.all_gather(w_in_rows, 'mp', axis=1, tiled=True)]
    ppermute x0 -> x15, waiting for transfers between devices: none -> 9.37 us  [the longest x8 7.32 us: collect(): lower.append(lax.ppermute(lower[-1] if lower else x, axis, pairs))]
    reshape x0 -> x5, local copies, waits for them, and re-layouts: none -> 8.61 us  [the longest x3 7.13 us: full_front(): (embedded.reshape(samples_here, tok_sample, -1) + prompt_cond[:, None, :]...]
    reduce_sum x4 -> x0, local copies, waits for them, and re-layouts: 7.12 us -> none  [sum_at_owner(): return arrived.astype(jnp.float32).sum(axis=0)]
    unnamed x41 -> x61, local copies, waits for them, and re-layouts: 4.57 us -> 11.5 us
    add x1 -> x3, other arithmetic: 0.06 us -> 6.5 us  [full_front(): (embedded.reshape(samples_here, tok_sample, -1) + prompt_cond[:, None, :]...]
  transfers between devices with their start and end apart: 6 -> 21, of which waited for: 4 -> 10; matrix products, arithmetic and copies ran while one was open for 1% -> 3% of each run, Pallas kernels for 0% -> 0%
where the time goes in v1:
time: 587 us; the launch traced here: 585 us
  blocking collectives  325 us (55%)
  waiting for transfers between devices  103 us (18%)
  matrix products  43.5 us (7%)
  local copies, waits for them, and re-layouts  41.4 us (7%)
  starting transfers between devices  36.8 us (6%)
  other arithmetic  19.8 us (3%)
  between operations  15.4 us (3%)
    all_to_all x3, blocking collectives, sum_at_owner(): lax.all_to_all(blocks, axis, split_axis=0, concat_axis=0, tiled=True)  128 us
    all_to_all x3, waiting for transfers between devices, sent_to_all(): return lax.all_to_all(copies, axis, split_axis=0, concat_axis=0, tiled=True)  77.4 us
    all_to_all x2, blocking collectives, sent_to_all(): return lax.all_to_all(copies, axis, split_axis=0, concat_axis=0, tiled=True)  62.5 us
    unnamed x1, blocking collectives  28 us
    psum x1, blocking collectives, decode_tile(): lax.psum((jnp.sum(grouped, axis=(1, 3)), jnp.sum(grouped * grouped, axis=...  25.8 us
    all_gather x1, blocking collectives, per_device(): lax.all_gather(w_in, 'segment', axis=0, tiled=True)  23.2 us
    all_gather x1, blocking collectives, per_device(): lax.all_gather(w_out, 'segment', axis=1, tiled=True)  22.4 us
    dot_general x4, matrix products, per_device(): jnp.dot(act, w_down_cols, preferred_element_type=jnp.float32)  19.3 us
  transfers between devices with their start and end apart: 21, of which 10 were waited for; matrix products, arithmetic and copies ran while one was open for 3% of the time, Pallas kernels for 0%

profile of v1, /device:TPU:8, one launch (start us, length us, event | category | flops | bytes accessed | tf_op | source)
XLA Modules:
  0.0 585.0 jit_solution(7781824879629960473)
XLA Ops:
  7.9 23.2 %all-gather = bf16[16,4,96]{2,1,0:T(4,128)(2,1)S(1)} all-gather(bf16[1,4,96]{2,1,0:T(4,128)(2,1)} %bitcast.281), channel_id=1, replica_groups=mesh['segment'=16,'mp'=16] {'segment'}, dimensions={0}, use_global_device_ids=true | all-gather | bytes 13056 | tf_op jit(solution)/shard_map/all_gather | solution.py:157
  31.2 4.4 collective-permute-done
  44.3 18.4 %all-gather.1 = bf16[16,2,96]{2,1,0:T(2,128)(2,1)S(1)} all-gather(bf16[1,2,96]{2,1,0:T(2,128)(2,1)} %bitcast.283), channel_id=1, replica_groups=mesh['segment'=16,'mp'=16] {'segment'}, dimensions={0}, use_global_device_ids=true | all-gather | bytes 6528 | tf_op jit(solution)/shard_map/all_gather | solution.py:161
  63.2 16.9 %all-gather.2 = bf16[16,96,32]{1,2,0:T(8,128)(2,1)S(1)} all-gather(bf16[1,96,32]{1,2,0:T(8,128)(2,1)S(1)} %bitcast.280), channel_id=1, replica_groups=mesh['segment'=16,'mp'=16] {'mp'}, dimensions={0}, use_global_device_ids=true | all-gather | bytes 104448 | tf_op jit(solution)/shard_map/all_gather | solution.py:175
  96.6 28.0 %all-reduce.6 = (bf16[1536]{0:T(1024)(128)(2,1)S(1)}, bf16[1536]{0:T(1024)(128)(2,1)}) all-reduce(bf16[1536]{0:T(1024)(128)(2,1)S(1)} %dynamic-update-slice, bf16[1536]{0:T(1024)(128)(2,1)S(1)} %dynamic-update-slice.1), channel_id=1, replica_groups=mesh['segment'=16,'mp'=16] {'mp'}, use_global_device_ids=true, to_apply=%add.3 | all-reduce | flops 3072 | bytes 12288
  134.7 4.8 convolution_convert_fusion.4
  142.2 5.1 all-to-all-start
  147.3 22.4 %all-gather.3 = bf16[16,4,96]{2,1,0:T(4,128)(2,1)S(1)} all-gather(bf16[1,4,96]{2,1,0:T(4,128)(2,1)S(1)} %bitcast.282), channel_id=1, replica_groups=mesh['segment'=16,'mp'=16] {'segment'}, dimensions={0}, use_global_device_ids=true | all-gather | bytes 13056 | tf_op jit(solution)/shard_map/all_gather | solution.py:160
  169.7 15.5 %all-to-all-done = bf16[16,512,96]{1,2,0:T(8,128)(2,1)} async-done(((bf16[16,512,96]{1,2,0:T(8,128)(2,1)}), bf16[16,512,96]{1,2,0:T(8,128)(2,1)}, u32[]{:S(2)}, u32[]{:S(2)}) %all-to-all-start) | async-done | bytes 1572896 | tf_op jit(solution)/shard_map/all_to_all | solution.py:45
  188.1 4.8 all-to-all-start.1
  195.4 24.2 %all-to-all-done.1 = bf16[16,512,64]{1,2,0:T(8,128)(2,1)S(1)} async-done(((bf16[16,512,64]{1,2,0:T(8,128)(2,1)}), bf16[16,512,64]{1,2,0:T(8,128)(2,1)S(1)}, u32[]{:S(2)}, u32[]{:S(2)}) %all-to-all-start.1) | async-done | bytes 1048608 | tf_op jit(solution)/shard_map/all_to_all | solution.py:51
  234.4 4.8 convolution_convert_fusion.3
  240.9 43.1 %all_to_all.45 = bf16[16,512,96]{1,2,0:T(8,128)(2,1)S(1)} all-to-all(bf16[16,512,96]{1,2,0:T(8,128)(2,1)S(1)} %bitcast.262), channel_id=1, replica_groups=mesh['segment'=16,'mp'=16] {'mp'}, dimensions={0} | all-to-all | bytes 3145728 | tf_op jit(solution)/shard_map/all_to_all | solution.py:45
  285.5 31.2 %all_to_all.46 = bf16[16,512,64]{1,2,0:T(8,128)(2,1)S(1)} all-to-all(bf16[16,512,64]{1,2,0:T(8,128)(2,1)S(1)} %broadcast_in_dim.19), channel_id=1, replica_groups=mesh['segment'=16,'mp'=16] {'mp'}, dimensions={0} | all-to-all | bytes 2097152 | tf_op jit(solution)/shard_map/all_to_all | solution.py:51
  325.3 4.8 convolution_convert_fusion.2
  331.8 42.5 %all_to_all.47 = bf16[16,512,96]{1,2,0:T(8,128)(2,1)S(1)} all-to-all(bf16[16,512,96]{1,2,0:T(8,128)(2,1)S(1)} %bitcast.263), channel_id=1, replica_groups=mesh['segment'=16,'mp'=16] {'mp'}, dimensions={0} | all-to-all | bytes 3145728 | tf_op jit(solution)/shard_map/all_to_all | solution.py:45
  375.8 31.3 %all_to_all.48 = bf16[16,512,64]{1,2,0:T(8,128)(2,1)S(1)} all-to-all(bf16[16,512,64]{1,2,0:T(8,128)(2,1)S(1)} %broadcast_in_dim.20), channel_id=1, replica_groups=mesh['segment'=16,'mp'=16] {'mp'}, dimensions={0} | all-to-all | bytes 2097152 | tf_op jit(solution)/shard_map/all_to_all | solution.py:51
  417.3 4.8 convolution_convert_fusion.1
  423.9 42.5 %all_to_all.49 = bf16[16,512,96]{1,2,0:T(8,128)(2,1)S(1)} all-to-all(bf16[16,512,96]{1,2,0:T(8,128)(2,1)S(1)} %bitcast.264), channel_id=1, replica_groups=mesh['segment'=16,'mp'=16] {'mp'}, dimensions={0} | all-to-all | bytes 3145728 | tf_op jit(solution)/shard_map/all_to_all | solution.py:45
  468.8 4.2 all-to-all-start.7
  473.0 26.6 %all-to-all-done.7 = bf16[16,512,64]{1,2,0:T(8,128)(2,1)S(1)} async-done(((bf16[16,512,64]{1,2,0:T(8,128)(2,1)}), bf16[16,512,64]{1,2,0:T(8,128)(2,1)S(1)}, u32[]{:S(2)}, u32[]{:S(2)}) %all-to-all-start.7) | async-done | bytes 1048608 | tf_op jit(solution)/shard_map/all_to_all | solution.py:51
  503.5 25.8 %all-reduce.5 = (f32[8,32]{1,0:T(8,128)S(1)}, f32[8,32]{1,0:T(8,128)S(1)}) all-reduce(f32[8,32]{1,0:T(8,128)S(1)} %reduce_sum.197, f32[8,32]{1,0:T(8,128)S(1)} %reduce_sum.194), channel_id=1, replica_groups=mesh['segment'=16,'mp'=16] {'mp'}, use_global_device_ids=true, to_apply=%region_21.22 | all-reduce | flops 512 | bytes 4096 | tf_op jit(solution)/shard_map/psum | solution.py:90
  543.2 7.2 %all-to-all-start.8 = ((bf16[16,8,8192]{2,1,0:T(8,128)(2,1)}), bf16[16,8,8192]{2,1,0:T(8,128)(2,1)S(1)}, u32[]{:S(2)}, u32[]{:S(2)}) async-start(bf16[16,8,8192]{2,1,0:T(8,128)(2,1)} %broadcast_in_dim.24), calls=%async_computation.8 | async-start | bytes 4194304 | tf_op jit(solution)/shard_map/all_to_all | solution.py:51
  550.3 26.6 %all-to-all-done.8 = bf16[16,8,8192]{2,1,0:T(8,128)(2,1)S(1)} async-done(((bf16[16,8,8192]{2,1,0:T(8,128)(2,1)}), bf16[16,8,8192]{2,1,0:T(8,128)(2,1)S(1)}, u32[]{:S(2)}, u32[]{:S(2)}) %all-to-all-start.8) | async-done | bytes 2097184 | tf_op jit(solution)/shard_map/all_to_all | solution.py:51
  (201 shorter events, 106.6 us)
Async XLA Ops:
  7.2 127.5 %all-gather.7.cloned.1.call-start = ((), (), s32[]{:S(2)}) async-start(), calls=%async_computation.9 | async-start | bytes 1253376 | tf_op jit(solution)/shard_map/all_gather | solution.py:158
  7.9 126.8 %all-gather.9.cloned.1.call-start = ((), (), s32[]{:S(2)}) async-start(), calls=%async_computation.10 | async-start | bytes 1253376 | tf_op jit(solution)/shard_map/all_gather | solution.py:159
  31.2 4.4 collective-permute-start
  35.5 4.4 collective-permute-start.1
  35.5 4.4 collective-permute-start.8
  39.9 4.4 collective-permute-start.2
  39.9 22.7 %collective-permute-start.9 = (bf16[64,96]{1,0:T(8,128)(2,1)S(1)}, bf16[64,96]{1,0:T(8,128)(2,1)S(1)}, u32[]{:S(2)}, u32[]{:S(2)}) collective-permute-start(bf16[64,96]{1,0:T(8,128)(2,1)S(1)} %collective-permute-done.8), channel_id=1, source_target_pairs={{1,0},{2,1},{3,2},{4,3},{5,4},{6,5},{7,6},{8,7},{9,8},{10,9},{11,1... | collective-permute-start | bytes 36872 | tf_op jit(solution)/shard_map/ppermute | solution.py:31
  44.3 18.5 %collective-permute-start.3 = (bf16[64,96]{1,0:T(8,128)(2,1)S(1)}, bf16[64,96]{1,0:T(8,128)(2,1)S(1)}, u32[]{:S(2)}, u32[]{:S(2)}) collective-permute-start(bf16[64,96]{1,0:T(8,128)(2,1)S(1)} %collective-permute-done.2), channel_id=1, source_target_pairs={{0,1},{1,2},{2,3},{3,4},{4,5},{5,6},{6,7},{7,8},{8,9},{9,10},{10,1... | collective-permute-start | bytes 36872 | tf_op jit(solution)/shard_map/ppermute | solution.py:29
  62.7 17.6 %collective-permute-start.10 = (bf16[64,96]{1,0:T(8,128)(2,1)S(1)}, bf16[64,96]{1,0:T(8,128)(2,1)S(1)}, u32[]{:S(2)}, u32[]{:S(2)}) collective-permute-start(bf16[64,96]{1,0:T(8,128)(2,1)S(1)} %collective-permute-done.9), channel_id=1, source_target_pairs={{1,0},{2,1},{3,2},{4,3},{5,4},{6,5},{7,6},{8,7},{9,8},{10,9},{11,1... | collective-permute-start | bytes 36872 | tf_op jit(solution)/shard_map/ppermute | solution.py:31
  62.8 20.7 %collective-permute-start.4 = (bf16[64,96]{1,0:T(8,128)(2,1)S(1)}, bf16[64,96]{1,0:T(8,128)(2,1)S(1)}, u32[]{:S(2)}, u32[]{:S(2)}) collective-permute-start(bf16[64,96]{1,0:T(8,128)(2,1)S(1)} %collective-permute-done.3), channel_id=1, source_target_pairs={{0,1},{1,2},{2,3},{3,4},{4,5},{5,6},{6,7},{7,8},{8,9},{9,10},{10,1... | collective-permute-start | bytes 36872 | tf_op jit(solution)/shard_map/ppermute | solution.py:29
  80.3 4.6 collective-permute-start.11
  83.5 4.4 collective-permute-start.5
  84.9 4.4 collective-permute-start.12
  87.8 4.5 collective-permute-start.6
  89.3 38.9 %collective-permute-start.13 = (bf16[64,96]{1,0:T(8,128)(2,1)S(1)}, bf16[64,96]{1,0:T(8,128)(2,1)S(1)}, u32[]{:S(2)}, u32[]{:S(2)}) collective-permute-start(bf16[64,96]{1,0:T(8,128)(2,1)S(1)} %collective-permute-done.12), channel_id=1, source_target_pairs={{1,0},{2,1},{3,2},{4,3},{5,4},{6,5},{7,6},{8,7},{9,8},{10,9},{11,1... | collective-permute-start | bytes 36872 | tf_op jit(solution)/shard_map/ppermute | solution.py:31
  92.3 35.9 %collective-permute-start.7 = (bf16[64,96]{1,0:T(8,128)(2,1)}, bf16[64,96]{1,0:T(8,128)(2,1)}, u32[]{:S(2)}, u32[]{:S(2)}) collective-permute-start(bf16[64,96]{1,0:T(8,128)(2,1)} %collective-permute-done.6), channel_id=1, source_target_pairs={{0,1},{1,2},{2,3},{3,4},{4,5},{5,6},{6,7},{7,8},{8,9},{9,10},{10,1... | collective-permute-start | bytes 36872 | tf_op jit(solution)/shard_map/ppermute | solution.py:29
  128.2 1.6 collective-permute-start.14
  142.2 43.0 %all-to-all-start = ((bf16[16,512,96]{1,2,0:T(8,128)(2,1)}), bf16[16,512,96]{1,2,0:T(8,128)(2,1)}, u32[]{:S(2)}, u32[]{:S(2)}) async-start(bf16[16,512,96]{1,2,0:T(8,128)(2,1)} %bitcast.261), calls=%async_computation | async-start | bytes 3145728 | tf_op jit(solution)/shard_map/all_to_all | solution.py:45
  188.1 31.5 %all-to-all-start.1 = ((bf16[16,512,64]{1,2,0:T(8,128)(2,1)}), bf16[16,512,64]{1,2,0:T(8,128)(2,1)S(1)}, u32[]{:S(2)}, u32[]{:S(2)}) async-start(bf16[16,512,64]{1,2,0:T(8,128)(2,1)} %broadcast_in_dim.18), calls=%async_computation.1 | async-start | bytes 2097152 | tf_op jit(solution)/shard_map/all_to_all | solution.py:51
  466.4 33.4 %copy-start.10 = (f32[512,64]{0,1:T(8,128)S(1)}, f32[512,64]{0,1:T(8,128)}, u32[]{:S(2)}) copy-start(f32[512,64]{0,1:T(8,128)} %get-tuple-element.11) | copy-start | bytes 393220
  467.7 33.4 %copy-start.11 = (bf16[3,3,16,512]{3,2,1,0:T(8,128)(2,1)S(1)}, bf16[3,3,16,512]{3,2,1,0:T(8,128)(2,1)}, u32[]{:S(2)}) copy-start(bf16[3,3,16,512]{3,2,1,0:T(8,128)(2,1)} %param.25) | copy-start | bytes 442372
  468.8 30.8 %all-to-all-start.7 = ((bf16[16,512,64]{1,2,0:T(8,128)(2,1)}), bf16[16,512,64]{1,2,0:T(8,128)(2,1)S(1)}, u32[]{:S(2)}, u32[]{:S(2)}) async-start(bf16[16,512,64]{1,2,0:T(8,128)(2,1)} %broadcast_in_dim.21), calls=%async_computation.7 | async-start | bytes 2097152 | tf_op jit(solution)/shard_map/all_to_all | solution.py:51
  541.6 35.4 %copy-start.18 = (s32[128]{0:T(128)S(1)}, s32[128]{0:T(128)}, u32[]{:S(2)}) copy-start(s32[128]{0:T(128)} %param.17) | copy-start | bytes 1540
  543.2 33.8 %all-to-all-start.8 = ((bf16[16,8,8192]{2,1,0:T(8,128)(2,1)}), bf16[16,8,8192]{2,1,0:T(8,128)(2,1)S(1)}, u32[]{:S(2)}, u32[]{:S(2)}) async-start(bf16[16,8,8192]{2,1,0:T(8,128)(2,1)} %broadcast_in_dim.24), calls=%async_computation.8 | async-start | bytes 4194304 | tf_op jit(solution)/shard_map/all_to_all | solution.py:51
  (16 other events, 196.1 us)
Sparse Core Ops, SparseCore 0:
  10.5 50.6 all-gather.6
  63.7 47.4 all-gather.8
